TPU v7x, 32 devices: a whole 2x2x4 slice. The times are simulated.
32 devices in a mesh: groups: 2 (over y), nodes: 4 (over z), classes: 4 (over x, core).
Axes of the slice: x: 2, y: 2, z: 4, core: 2. Of those that a mesh axis runs over, the one named last changes fastest.
Arguments:
- scores: float32 [1024, 8192], P('classes', ('groups', 'nodes')), parts along dimension 1, may hold values from 0.2 to 15, as said below
- prior: float32 [1024, 8192], P('classes', ('groups', 'nodes')), parts along dimension 1, may hold values from 0 to 2
- tiles: bfloat16 [8, 4, 6, 128, 128], P(('groups', 'nodes')), parts along dimension 0, may hold values from 0 to 0.015625
- col_tile: int32 [8, 4, 6], P(('groups', 'nodes')), parts along dimension 0, may hold values from 0 to 7
- row_tile: int32 [8, 4, 6], P('groups', 'nodes'), parts along dimension 0, may hold values from 0 to 7
- counts: int32 [8, 4], P('groups', 'nodes'), parts along dimension 0, may hold values from 1 to 6, as said below
- seed_mask: int32 [8192], P(('groups', 'nodes')), parts along dimension 0, may hold values 0 or 1
Outputs:
- spread_scores: float32 [1024, 8192], P('classes', ('groups', 'nodes')), parts along dimension 1
There are 2 independent parts, one for each index of `groups`. A program takes and returns all parts, laid end to end along the dimension named above; each array names one. Nothing has to cross between parts.
Inputs may be any that keep to these rules, and one draw needn't show every extreme that they name: Each node's starting scores are positive. counts[p, d] slots of the 6 from partition p to partition d are used; in every draw some partition receives 6 from every partition.
All inputs are finite; a program needn't handle non-finite values. No bound on the sum of `seed_mask` on one device may be relied on, other than what follows from the above.
Results may differ from a plain program's by a relative error of at most 0.0003.
Values may be sent and summed in bfloat16 or wider, within the bound.
A program may use at most 64 MiB of HBM per device.

v0:
```python
import jax
import jax.numpy as jnp
from jax import lax
from jax.sharding import PartitionSpec as P

CLASSES = 1024
ITERS = 2


def body(scores, prior, tiles, col_tile, row_tile, counts, seed_mask):
    tiles = tiles[0]
    col_tile = col_tile[0]
    incoming_rows = row_tile[:, 0]
    incoming_counts = counts[:, 0]
    tile_width = tiles.shape[-1]
    class_rows = scores.shape[0]
    block_count = scores.shape[1] // tile_width
    usable = lax.broadcasted_iota(jnp.int32, incoming_rows.shape, 1) < incoming_counts[:, None]
    target_pick = jax.nn.one_hot(incoming_rows, block_count, dtype=jnp.bfloat16) * usable[
        ..., None
    ].astype(jnp.bfloat16)
    source_pick = jax.nn.one_hot(col_tile, block_count, dtype=jnp.bfloat16)
    seeded = seed_mask.astype(jnp.float32)[None, :]
    scores_now = scores
    for sweep in range(ITERS):
        field_low = scores_now.astype(jnp.bfloat16).reshape(class_rows, block_count, tile_width)
        picked = jnp.einsum(
            "pse,cek->psck", source_pick, field_low, preferred_element_type=jnp.float32
        ).astype(jnp.bfloat16)
        products = jnp.einsum(
            "psck,pskj->pscj", picked, tiles, preferred_element_type=jnp.float32
        ).astype(jnp.bfloat16)
        arrived = lax.all_to_all(products, "nodes", split_axis=0, concat_axis=0, tiled=True)
        gathered = jnp.einsum(
            "pse,pscj->cej", target_pick, arrived, preferred_element_type=jnp.float32
        )
        tallied = scores_now + gathered.reshape(class_rows, block_count * tile_width)
        node_total = lax.psum(jnp.sum(tallied, axis=0), "classes")
        normed = CLASSES * tallied / node_total[None, :]
        scores_now = normed + 0.5 * seeded * (prior - normed)
    return scores_now


def solution(mesh):
    placed = (
        P("classes", ("groups", "nodes")),
        P("classes", ("groups", "nodes")),
        P(("groups", "nodes"), None, None, None, None),
        P(("groups", "nodes"), None, None),
        P("groups", "nodes", None),
        P("groups", "nodes"),
        P(("groups", "nodes")),
    )
    return jax.shard_map(
        body,
        mesh=mesh,
        in_specs=placed,
        out_specs=P("classes", ("groups", "nodes")),
        check_vma=False,
    )
```

profile of v0, /device:TPU:0, one launch (start us, length us, event | category | flops | bytes accessed | tf_op | source)
XLA Modules:
  0.0 110.3 jit_solution(9688116579340568631)
XLA Ops:
  0.0 0.0 copy-start
  0.0 0.0 copy-start.6
  0.0 1.4 %convert_bitcast_fusion.1 = bf16[32,8,8,128]{3,1,2,0:T(8,128)(2,1)S(1)} fusion(f32[256,1024]{1,0:T(8,128)} %param.7), kind=kLoop, calls=%fused_computation.15 | loop fusion | flops 262144 | bytes 1572864
  1.4 0.1 copy.15
  1.5 0.0 copy-done.6
  1.5 0.6 fusion.11
  2.1 0.0 copy-done
  2.1 1.7 %convolution_convert_fusion.1 = bf16[4,6,256,128]{3,2,1,0:T(8,128)(2,1)} fusion(bf16[4,6,256,128]{3,1,2,0:T(8,128)(2,1)S(1)} %fusion.11, bf16[1,4,6,128,128]{4,3,2,1,0:T(8,128)(2,1)S(1)} %copy-done), kind=kOutput, calls=%fused_computation.7 | convolution fusion | flops 202113024 | bytes 3932160 | tf_op jit(solution)/shard_map/psck,pskj->pscj/dot_general | solution.py:30
  3.9 0.0 copy-start.8
  3.9 0.0 copy-start.7
  3.9 0.0 copy-start.5
  3.9 6.5 %all-to-all-start = ((bf16[4,6,256,128]{3,2,1,0:T(8,128)(2,1)}), bf16[4,6,256,128]{3,2,1,0:T(8,128)(2,1)S(1)}, u32[]{:S(2)}, u32[]{:S(2)}) async-start(bf16[4,6,256,128]{3,2,1,0:T(8,128)(2,1)} %convolution_convert_fusion.1), calls=%async_computation | async-start | bytes 3145728 | tf_op jit(solution)/shard_map/all_to_all | solution.py:33
  10.3 0.0 copy-start.1
  10.3 0.0 copy-done.8
  10.3 0.1 fusion.25
  10.4 0.0 copy-done.7
  10.4 36.9 %all-to-all-done = bf16[4,6,256,128]{3,2,1,0:T(8,128)(2,1)S(1)} async-done(((bf16[4,6,256,128]{3,2,1,0:T(8,128)(2,1)}), bf16[4,6,256,128]{3,2,1,0:T(8,128)(2,1)S(1)}, u32[]{:S(2)}, u32[]{:S(2)}) %all-to-all-start) | async-done | bytes 1572896 | tf_op jit(solution)/shard_map/all_to_all | solution.py:33
  47.3 0.0 copy-start.3
  47.3 1.2 %copy-done.3 = bf16[4,6,256,128]{3,2,1,0:T(8,128)(2,1)} copy-done((bf16[4,6,256,128]{3,2,1,0:T(8,128)(2,1)}, bf16[4,6,256,128]{3,2,1,0:T(8,128)(2,1)S(1)}, u32[]{:S(2)}) %copy-start.3) | copy-done | bytes 1572888
  48.4 0.0 copy-done.5
  48.4 2.9 %fusion.2 = f32[256,128,8,1]{1,2,3,0:T(8,128)S(1)} fusion(bf16[4,6,256,128]{3,2,1,0:T(8,128)(2,1)} %copy-done.3, s32[4,6]{1,0:T(4,128)S(1)} %bitcast.59, bf16[4,6]{1,0:T(4,128)(2,1)S(1)} %fusion.25), kind=kOutput, calls=%fused_computation.4 | convolution fusion | flops 12583296 | bytes 2621584 | tf_op jit(solution)/shard_map/pse,pscj->cej/dot_general | solution.py:34
  51.4 0.0 copy-done.1
  51.4 0.3 fusion.6
  51.7 5.8 %psum.14 = f32[1024]{0:T(1024)S(1)} all-reduce(f32[1024]{0:T(1024)S(1)} %fusion.6), channel_id=1, replica_groups=mesh['groups'=2,'nodes'=4,'classes'=4] {'classes'}, use_global_device_ids=true, to_apply=%region_1.2 | all-reduce | flops 1024 | bytes 8192 | tf_op jit(solution)/shard_map/psum | solution.py:38
  57.5 1.7 %convert_bitcast_fusion = (bf16[32,8,8,128]{3,1,2,0:T(8,128)(2,1)S(1)}, f32[256,1024]{1,0:T(8,128)S(1)}) fusion(f32[256,1024]{1,0:T(8,128)} %param.8, f32[1024]{0:T(1024)S(1)} %convert_multiply_fusion, f32[1024]{0:T(1024)S(1)} %psum.14, f32[256,1024]{1,0:T(8,128)S(1)} %copy-done.1, f32[32,8,8,128]{3,2,1,0:T(8,128)S(1)} %bitcast.56), kind=kLoop, calls=%fused_computation.14 | loop fusion | flops 1835008 | bytes 4726784
  59.2 0.0 copy-start.2
  59.2 0.1 copy.17
  59.3 0.6 fusion.9
  60.0 0.6 convolution_convert_fusion
  60.5 39.6 %all_to_all.10 = bf16[4,6,256,128]{3,2,1,0:T(8,128)(2,1)S(1)} all-to-all(bf16[4,6,256,128]{3,2,1,0:T(8,128)(2,1)S(1)} %convolution_convert_fusion), channel_id=1, replica_groups=mesh['groups'=2,'nodes'=4,'classes'=4] {'nodes'}, dimensions={0} | all-to-all | bytes 3145728 | tf_op jit(solution)/shard_map/all_to_all | solution.py:33
  100.1 0.0 copy-start.4
  100.1 1.6 %fusion = f32[256,128,8,1]{1,2,3,0:T(8,128)S(1)} fusion(bf16[4,6,256,128]{3,2,1,0:T(8,128)(2,1)S(1)} %all_to_all.10, s32[4,6]{1,0:T(4,128)S(1)} %bitcast.60, bf16[4,6]{1,0:T(4,128)(2,1)S(1)} %fusion.25), kind=kOutput, calls=%fused_computation.2 | convolution fusion | flops 12583296 | bytes 2621584 | tf_op jit(solution)/shard_map/pse,pscj->cej/dot_general | solution.py:34
  101.7 0.0 copy-done.2
  101.7 0.3 fusion.7
  102.0 5.7 %psum.15 = f32[1024]{0:T(1024)S(1)} all-reduce(f32[1024]{0:T(1024)S(1)} %fusion.7), channel_id=1, replica_groups=mesh['groups'=2,'nodes'=4,'classes'=4] {'classes'}, use_global_device_ids=true, to_apply=%region_3.4 | all-reduce | flops 1024 | bytes 8192 | tf_op jit(solution)/shard_map/psum | solution.py:38
  107.6 0.0 copy-done.4
  107.6 2.7 %multiply_add_fusion = f32[256,1024]{1,0:T(8,128)} fusion(f32[256,1024]{1,0:T(8,128)S(1)} %copy-done.4, f32[1024]{0:T(1024)S(1)} %psum.15, f32[1024]{0:T(1024)S(1)} %convert_multiply_fusion, f32[256,1024]{1,0:T(8,128)} %copy-done.2, f32[32,8,8,128]{3,2,1,0:T(8,128)S(1)} %bitcast.54), kind=kLoop, calls=%fused_computation.10 | loop fusion | flops 1572864 | bytes 4202496 | tf_op jit(solution)/shard_map/add | solution.py:40
  (1 shorter events, 0.0 us)
Async XLA Ops:
  0.0 2.1 %copy-start = (bf16[1,4,6,128,128]{4,3,2,1,0:T(8,128)(2,1)S(1)}, bf16[1,4,6,128,128]{4,3,2,1,0:T(8,128)(2,1)}, u32[]{:S(2)}) copy-start(bf16[1,4,6,128,128]{4,3,2,1,0:T(8,128)(2,1)} %param.9) | copy-start | bytes 2359300
  0.0 1.5 %copy-start.6 = (s32[1,4,6]{2,1,0:T(4,128)S(1)}, s32[1,4,6]{2,1,0:T(4,128)}, u32[]{:S(2)}) copy-start(s32[1,4,6]{2,1,0:T(4,128)} %param.10) | copy-start | bytes 292
  3.9 6.5 %copy-start.8 = (s32[4,1]{0,1:T(1,128)S(1)}, s32[4,1]{0,1:T(1,128)}, u32[]{:S(2)}) copy-start(s32[4,1]{0,1:T(1,128)} %param.12) | copy-start | bytes 52
  3.9 6.5 %copy-start.7 = (s32[1024]{0:T(1024)S(1)}, s32[1024]{0:T(1024)}, u32[]{:S(2)}) copy-start(s32[1024]{0:T(1024)} %param.13) | copy-start | bytes 12292
  3.9 44.6 %copy-start.5 = (s32[4,1,6]{2,1,0:T(1,128)S(1)}, s32[4,1,6]{2,1,0:T(1,128)}, u32[]{:S(2)}) copy-start(s32[4,1,6]{2,1,0:T(1,128)} %param.11) | copy-start | bytes 292
  3.9 43.4 %all-to-all-start = ((bf16[4,6,256,128]{3,2,1,0:T(8,128)(2,1)}), bf16[4,6,256,128]{3,2,1,0:T(8,128)(2,1)S(1)}, u32[]{:S(2)}, u32[]{:S(2)}) async-start(bf16[4,6,256,128]{3,2,1,0:T(8,128)(2,1)} %convolution_convert_fusion.1), calls=%async_computation | async-start | bytes 3145728 | tf_op jit(solution)/shard_map/all_to_all | solution.py:33
  10.3 41.0 %copy-start.1 = (f32[256,1024]{1,0:T(8,128)S(1)}, f32[256,1024]{1,0:T(8,128)}, u32[]{:S(2)}) copy-start(f32[256,1024]{1,0:T(8,128)} %param.7) | copy-start | bytes 3145732
  47.3 1.2 %copy-start.3 = (bf16[4,6,256,128]{3,2,1,0:T(8,128)(2,1)}, bf16[4,6,256,128]{3,2,1,0:T(8,128)(2,1)S(1)}, u32[]{:S(2)}) copy-start(bf16[4,6,256,128]{3,2,1,0:T(8,128)(2,1)S(1)} %all-to-all-done) | copy-start | bytes 4718596
  59.2 42.4 %copy-start.2 = (f32[256,1024]{1,0:T(8,128)}, f32[256,1024]{1,0:T(8,128)S(1)}, u32[]{:S(2)}) copy-start(f32[256,1024]{1,0:T(8,128)S(1)} %get-tuple-element.6) | copy-start | bytes 3145732
  100.1 7.5 %copy-start.4 = (f32[256,1024]{1,0:T(8,128)S(1)}, f32[256,1024]{1,0:T(8,128)}, u32[]{:S(2)}) copy-start(f32[256,1024]{1,0:T(8,128)} %param.8) | copy-start | bytes 3145732
where the time goes:
time: 111 us; the launch traced here: 110 us
  blocking collectives  51.1 us (46%)
  waiting for transfers between devices  36.9 us (33%)
  matrix products  8 us (7%)
  other arithmetic  6.47 us (6%)
  starting transfers between devices  6.45 us (6%)
  local copies, waits for them, and re-layouts  1.38 us (1%)
    all_to_all x1, blocking collectives, body(): lax.all_to_all(products, 'nodes', split_axis=0, concat_axis=0, tiled=True)  39.6 us
    all_to_all x1, waiting for transfers between devices, body(): lax.all_to_all(products, 'nodes', split_axis=0, concat_axis=0, tiled=True)  36.9 us
    psum x2, blocking collectives, body(): node_total = lax.psum(jnp.sum(tallied, axis=0), 'classes')  11.5 us
    all_to_all x1, starting transfers between devices, body(): lax.all_to_all(products, 'nodes', split_axis=0, concat_axis=0, tiled=True)  6.45 us
    dot_general x2, matrix products, body(): jnp.einsum('pse,pscj->cej', target_pick, arrived, preferred_element_type=...  4.48 us
    unnamed x2, other arithmetic  3.12 us
    add x1, other arithmetic, body(): scores_now = normed + 0.5 * seeded * (prior - normed)  2.67 us
    dot_general x2, matrix products, body(): jnp.einsum('psck,pskj->pscj', picked, tiles, preferred_element_type=jnp.f...  2.28 us
  transfers between devices with their start and end apart: 1, of which 1 were waited for; matrix products, arithmetic and copies ran while one was open for 0% of the time, Pallas kernels for 0%

commit v1 on v0

--- a/solution.py
+++ b/solution.py
@@ -1,10 +1,17 @@
+import functools
+
 import jax
 import jax.numpy as jnp
 from jax import lax
+from jax.experimental import pallas as pl
+from jax.experimental.pallas import tpu as pltpu
 from jax.sharding import PartitionSpec as P
 
 CLASSES = 1024
 ITERS = 2
+MESH = pl.DeviceIdType.MESH
+F32 = jnp.float32
+I32 = jnp.int32
 
 
 def body(scores, prior, tiles, col_tile, row_tile, counts, seed_mask):
@@ -41,6 +48,382 @@
     return scores_now
 
 
+def pack(codes):
+    half = codes.shape[0] // 2
+    return lax.bitwise_or(codes[:half], lax.shift_left(codes[half:], jnp.int32(16)))
+
+
+def unpack(words):
+    low = lax.bitwise_and(words, jnp.int32(0xFFFF))
+    high = lax.shift_right_logical(words, jnp.int32(16))
+    return jnp.concatenate([low, high], axis=0)
+
+
+def encode_scores(x):
+    step = jnp.full_like(x, 65536.0)
+    octave = jnp.full(x.shape, -8192, I32)
+    edge, scale = 0.25, 32768.0
+    for level in range(7):
+        above = x >= edge
+        step = jnp.where(above, scale, step)
+        octave = jnp.where(above, level * 8192, octave)
+        edge, scale = edge * 2.0, scale * 0.5
+    return (x * step).astype(I32) + octave
+
+
+def decode_scores(codes):
+    octave = lax.shift_right_logical(codes, jnp.int32(13))
+    mantissa = lax.bitwise_and(codes, jnp.int32(8191)).astype(F32) + 8192.5
+    power = lax.shift_left(jnp.full_like(codes, 1), octave).astype(F32)
+    return mantissa * (power * (1.0 / 65536.0))
+
+
+def kernel(
+    N, C, NB, CAP, RT,
+    scores, prior, tiles, info, out,
+    words, rx_words, pwords, rx_pwords, owords, rx_owords,
+    all_tiles, field, low, votes, rx_info, sm,
+    sums, rx_sums, csums, rx_csums, total, side, rx_side, osum, rx_osum, mine,
+    local_sem, sm_sem,
+    info_s, info_r, tz_s, tz_r, tx_s, tx_r, tc_s, tc_r, td_s, td_r,
+    sc_s, sc_r, pr_s, pr_r, c1_s, c1_r, z1_s, z1_r, sd_s, sd_r, o_s, o_r, c2_s, c2_r,
+):
+    n = lax.axis_index("nodes")
+    c = lax.axis_index("classes")
+    SL = N * CAP
+    HR = RT // 2
+
+    def znode(k):
+        return lax.rem(n + k, N)
+
+    def zfrom(k):
+        return lax.rem(n - k + N, N)
+
+    def cnode(k):
+        return lax.rem(c + k, C)
+
+    def cfrom(k):
+        return lax.rem(c - k + C, C)
+
+    xpeer = lax.rem(c + 2, C)
+    kpeer = c + 1 - 2 * lax.rem(c, 2)
+    xkpeer = lax.rem(kpeer + 2, C)
+    order = [2, 1, 3]
+
+    def remote(src, dst, s, r, **to):
+        return pltpu.make_async_remote_copy(
+            src_ref=src, dst_ref=dst, send_sem=s, recv_sem=r, device_id=to, device_id_type=MESH
+        )
+
+    barrier = pltpu.get_barrier_semaphore()
+    for k in range(1, N):
+        pl.semaphore_signal(barrier, inc=1, device_id={"nodes": znode(k)}, device_id_type=MESH)
+    for k in range(1, C):
+        pl.semaphore_signal(barrier, inc=1, device_id={"classes": cnode(k)}, device_id_type=MESH)
+
+    own_tiles = pltpu.make_async_copy(tiles, all_tiles.at[n], local_sem)
+    own_tiles.start()
+    rx_info[n] = info[...]
+
+    def code_scores(d, carry):
+        rows = pl.ds(pl.multiple_of(d * RT, RT), RT)
+        for b in range(NB):
+            words[d, b] = pack(encode_scores(scores[rows, b * 128:(b + 1) * 128]))
+        return carry
+
+    lax.fori_loop(0, N, code_scores, 0)
+    pl.semaphore_wait(barrier, N - 1 + C - 1)
+
+    infos = [remote(info, rx_info.at[n], info_s.at[k], info_r.at[k], nodes=znode(k)) for k in order]
+    tzs = [
+        remote(tiles.at[c], all_tiles.at[n, c], tz_s.at[k], tz_r.at[k], nodes=znode(k))
+        for k in order
+    ]
+    scs = [
+        remote(words.at[znode(k)], rx_words.at[n], sc_s.at[k], sc_r.at[k], nodes=znode(k))
+        for k in order
+    ]
+    for copy in infos + tzs + scs:
+        copy.start()
+
+    def code_prior(d, carry):
+        rows = pl.ds(pl.multiple_of(d * RT, RT), RT)
+        for b in range(NB):
+            pwords[d, b] = pack(
+                (prior[rows, b * 128:(b + 1) * 128] * 32767.5 + 0.5).astype(I32)
+            )
+        return carry
+
+    lax.fori_loop(0, N, code_prior, 0)
+    prs = [
+        remote(pwords.at[znode(k)], rx_pwords.at[n], pr_s.at[k], pr_r.at[k], nodes=znode(k))
+        for k in order
+    ]
+    for copy in prs:
+        copy.start()
+
+    own_rows = pl.ds(pl.multiple_of(n * RT, RT), RT)
+    for b in range(NB):
+        x = scores[own_rows, b * 128:(b + 1) * 128]
+        field[n * NB + b] = x
+        low[n * NB + b] = x.astype(jnp.bfloat16)
+    rx_pwords[n] = pwords[n]
+
+    waiting = [1, 3, 2]
+    txs, tcs, tds = [], [], []
+    for k in waiting:
+        p = zfrom(k)
+        remote(tiles.at[c], all_tiles.at[p, c], tz_s.at[k], tz_r.at[k], nodes=p).wait_recv()
+        txs.append(
+            remote(all_tiles.at[p, c], all_tiles.at[p, c], tx_s.at[k], tx_r.at[k], classes=xpeer)
+        )
+        tcs.append(
+            remote(all_tiles.at[p, c], all_tiles.at[p, c], tc_s.at[k], tc_r.at[k], classes=kpeer)
+        )
+        txs[-1].start()
+        tcs[-1].start()
+    for k in order:
+        remote(info, rx_info.at[zfrom(k)], info_s.at[k], info_r.at[k], nodes=zfrom(k)).wait_recv()
+    to_sm = pltpu.make_async_copy(rx_info.at[:, 0:8], sm, sm_sem)
+    to_sm.start()
+    for k in waiting:
+        p = zfrom(k)
+        remote(words.at[p], rx_words.at[p], sc_s.at[k], sc_r.at[k], nodes=p).wait_recv()
+
+        def take_scores(b, carry):
+            x = decode_scores(unpack(rx_words[p, b]))
+            field[p * NB + b] = x
+            low[p * NB + b] = x.astype(jnp.bfloat16)
+            return carry
+
+        lax.fori_loop(0, NB, take_scores, 0)
+    to_sm.wait()
+    own_tiles.wait()
+    for k in waiting:
+        p = zfrom(k)
+        remote(
+            all_tiles.at[p, xpeer], all_tiles.at[p, xpeer], tx_s.at[k], tx_r.at[k], classes=xpeer
+        ).wait_recv()
+        tds.append(
+            remote(
+                all_tiles.at[p, xpeer], all_tiles.at[p, xpeer], td_s.at[k], td_r.at[k], classes=kpeer
+            )
+        )
+        tds[-1].start()
+    for k in waiting:
+        p = zfrom(k)
+        remote(
+            all_tiles.at[p, kpeer], all_tiles.at[p, kpeer], tc_s.at[k], tc_r.at[k], classes=kpeer
+        ).wait_recv()
+        remote(
+            all_tiles.at[p, xkpeer], all_tiles.at[p, xkpeer], td_s.at[k], td_r.at[k], classes=kpeer
+        ).wait_recv()
+
+    def cast_votes(d):
+        def one(p, carry):
+            for s in range(CAP):
+                col = sm[p, 0, d * CAP + s]
+                block = jnp.dot(
+                    low[p * NB + col], all_tiles[p, d, s], preferred_element_type=F32
+                )
+                votes[p * CAP + s] = block.astype(jnp.bfloat16).astype(F32)
+            return carry
+
+        lax.fori_loop(0, N, one, 0)
+
+    def tally(d, b):
+        acc = field[d * NB + b]
+        for i in range(SL):
+            p, s = i // CAP, i % CAP
+            row = sm[d, 0, SL + i]
+            hit = jnp.logical_and(row == b, s < sm[d, 0, 2 * SL + p])
+            acc = acc + jnp.where(hit, 1.0, 0.0).astype(F32) * votes[i]
+        return acc
+
+    def first(d, carry):
+        cast_votes(d)
+
+        def one(b, carry):
+            acc = tally(d, b)
+            field[d * NB + b] = acc
+            sums[d, pl.ds(b, 1)] = jnp.sum(acc, axis=0, keepdims=True)
+            return carry
+
+        lax.fori_loop(0, NB, one, 0)
+        return carry
+
+    lax.fori_loop(0, N, first, 0)
+
+    rx_sums[c] = sums[...]
+    c1s = [remote(sums, rx_sums.at[c], c1_s.at[k], c1_r.at[k], classes=cnode(k)) for k in range(1, C)]
+    for copy in c1s:
+        copy.start()
+    for k in range(1, C):
+        p = cfrom(k)
+        remote(sums, rx_sums.at[p], c1_s.at[k], c1_r.at[k], classes=p).wait_recv()
+    whole = rx_sums[0]
+    for k in range(1, C):
+        whole = whole + rx_sums[k]
+    csums[...] = whole
+    rx_csums[n] = whole
+    z1s = [remote(csums, rx_csums.at[n], z1_s.at[k], z1_r.at[k], nodes=znode(k)) for k in order]
+    for copy in z1s:
+        copy.start()
+    for k in waiting:
+        p = zfrom(k)
+        remote(csums, rx_csums.at[p], z1_s.at[k], z1_r.at[k], nodes=p).wait_recv()
+    whole = rx_csums[0]
+    for k in range(1, N):
+        whole = whole + rx_csums[k]
+    total[...] = 1024.0 / whole
+
+    def spread(p):
+        def one(b, carry):
+            seeded = 0.5 * rx_info[p, pl.ds(8 + b, 1)].astype(F32)
+            normed = field[p * NB + b] * total[p, pl.ds(b, 1)]
+            seeds = unpack(rx_pwords[p, b]).astype(F32) * (1.0 / 32767.5)
+            x = normed + seeded * (seeds - normed)
+            field[p * NB + b] = x
+            low[p * NB + b] = x.astype(jnp.bfloat16)
+            return carry
+
+        lax.fori_loop(0, NB, one, 0)
+
+    spread(n)
+    for k in waiting:
+        p = zfrom(k)
+        remote(pwords.at[p], rx_pwords.at[p], pr_s.at[k], pr_r.at[k], nodes=p).wait_recv()
+        spread(p)
+
+    sds, outs = [], []
+    for k in order:
+        d = znode(k)
+        cast_votes(d)
+
+        def one(b, carry):
+            acc = tally(d, b)
+            side[d, pl.ds(b, 1)] = jnp.sum(acc, axis=0, keepdims=True)
+            peak = jnp.maximum(jnp.max(acc, axis=0, keepdims=True), 1e-30)
+            side[d, pl.ds(8 + b, 1)] = peak * (1.0 / 65535.0)
+            owords[d, b] = pack((acc * (65535.0 / peak) + 0.5).astype(I32))
+            return carry
+
+        lax.fori_loop(0, NB, one, 0)
+        sds.append(remote(side.at[d], rx_side.at[n], sd_s.at[k], sd_r.at[k], nodes=d))
+        outs.append(remote(owords.at[d], rx_owords.at[n], o_s.at[k], o_r.at[k], nodes=d))
+        sds[-1].start()
+        outs[-1].start()
+    cast_votes(n)
+
+    def own(b, carry):
+        acc = tally(n, b)
+        mine[b] = acc
+        rx_side[n, pl.ds(b, 1)] = jnp.sum(acc, axis=0, keepdims=True)
+        return carry
+
+    lax.fori_loop(0, NB, own, 0)
+
+    for k in waiting:
+        p = zfrom(k)
+        remote(side.at[p], rx_side.at[p], sd_s.at[k], sd_r.at[k], nodes=p).wait_recv()
+    whole = rx_side[0, 0:8]
+    for p in range(1, N):
+        whole = whole + rx_side[p, 0:8]
+    osum[...] = whole
+    rx_osum[c] = whole
+    c2s = [remote(osum, rx_osum.at[c], c2_s.at[k], c2_r.at[k], classes=cnode(k)) for k in range(1, C)]
+    for copy in c2s:
+        copy.start()
+    for k in range(1, C):
+        p = cfrom(k)
+        remote(osum, rx_osum.at[p], c2_s.at[k], c2_r.at[k], classes=p).wait_recv()
+    whole = rx_osum[0]
+    for k in range(1, C):
+        whole = whole + rx_osum[k]
+    total[n] = 1024.0 / whole
+
+    def finish(p, b, tallied):
+        seeded = 0.5 * info[8 + b:9 + b].astype(F32)
+        rows = pl.ds(pl.multiple_of(p * RT, RT), RT)
+        normed = tallied * total[n, b:b + 1]
+        out[rows, b * 128:(b + 1) * 128] = normed + seeded * (
+            prior[rows, b * 128:(b + 1) * 128] - normed
+        )
+
+    for b in range(NB):
+        finish(n, b, mine[b])
+    for k in waiting:
+        p = zfrom(k)
+        remote(owords.at[p], rx_owords.at[p], o_s.at[k], o_r.at[k], nodes=p).wait_recv()
+        for b in range(NB):
+            codes = unpack(rx_owords[p, b]).astype(F32)
+            finish(p, b, codes * rx_side[p, 8 + b:9 + b])
+
+    for copy in infos + tzs + scs + prs + txs + tcs + tds + c1s + z1s + sds + outs + c2s:
+        copy.wait_send()
+
+
+def fits(mesh, scores, tiles):
+    return (
+        mesh.shape["nodes"] == 4
+        and mesh.shape["classes"] == 4
+        and scores.shape[1] // tiles.shape[-1] == 8
+        and tiles.shape[-1] == 128
+        and (scores.shape[0] // 4) % 16 == 0
+        and 2 * tiles.shape[1] * tiles.shape[2] + tiles.shape[1] <= 128
+    )
+
+
+def transposed(N, C, scores, prior, tiles, col_tile, row_tile, counts, seed_mask):
+    R = scores.shape[0]
+    CAP = tiles.shape[2]
+    TW = tiles.shape[-1]
+    NB = scores.shape[1] // TW
+    RT = R // N
+    SL = N * CAP
+    line = jnp.concatenate(
+        [col_tile[0].reshape(-1), row_tile[:, 0].reshape(-1), counts[:, 0]]
+    )
+    line = jnp.pad(line, (0, 8 * TW - line.shape[0])).reshape(8, TW)
+    info = jnp.concatenate([line, seed_mask.reshape(NB, TW)], axis=0)
+    V = pltpu.VMEM
+    words = V((N, NB, RT // 2, TW), I32)
+    dma = pltpu.SemaphoreType.DMA
+    pairs = [dma((4,)) for _ in range(24)]
+    vm = pl.BlockSpec(memory_space=pltpu.VMEM)
+    return pl.pallas_call(
+        functools.partial(kernel, N, C, NB, CAP, RT),
+        out_shape=jax.ShapeDtypeStruct(scores.shape, F32),
+        in_specs=[vm] * 4,
+        out_specs=vm,
+        scratch_shapes=[
+            words, words, words, words, words, words,
+            V((N, N, CAP, TW, TW), jnp.bfloat16),
+            V((N * NB, RT, TW), F32),
+            V((N * NB, RT, TW), jnp.bfloat16),
+            V((SL, RT, TW), F32),
+            V((N, 16, TW), I32),
+            pltpu.SMEM((N, 8, TW), I32),
+            V((N, NB, TW), F32),
+            V((C, N, NB, TW), F32),
+            V((N, NB, TW), F32),
+            V((N, N, NB, TW), F32),
+            V((N, NB, TW), F32),
+            V((N, 16, TW), F32),
+            V((N, 16, TW), F32),
+            V((NB, TW), F32),
+            V((C, NB, TW), F32),
+            V((NB, RT, TW), F32),
+            dma,
+            dma,
+            *pairs,
+        ],
+        compiler_params=pltpu.CompilerParams(
+            collective_id=0, has_side_effects=True, vmem_limit_bytes=40 * 1024 * 1024
+        ),
+    )(scores, prior, tiles[0], info)
+
+
 def solution(mesh):
     placed = (
         P("classes", ("groups", "nodes")),
@@ -51,8 +434,16 @@
         P("groups", "nodes"),
         P(("groups", "nodes")),
     )
+
+    def one_device(scores, prior, tiles, *rest):
+        if fits(mesh, scores, tiles):
+            return transposed(
+                mesh.shape["nodes"], mesh.shape["classes"], scores, prior, tiles, *rest
+            )
+        return body(scores, prior, tiles, *rest)
+
     return jax.shard_map(
-        body,
+        one_device,
         mesh=mesh,
         in_specs=placed,
         out_specs=P("classes", ("groups", "nodes")),

time: 111 us -> 78.8 us (0.71)
  the two profiles are of different devices: /device:TPU:0 before, /device:TPU:13 now
where the time goes in v1:
time: 78.8 us; the launch traced here: 78.5 us
  Pallas kernels  71.2 us (90%)
  local copies, waits for them, and re-layouts  6.52 us (8%)
    pallas_call x1, Pallas kernels, transposed(): pl.pallas_call(functools.partial(kernel, N, C, NB, CAP, RT), out_shape=ja...  71.2 us
    unnamed x16, local copies, waits for them, and re-layouts  6.35 us

profile of v1, /device:TPU:13, one launch (start us, length us, event | category | flops | bytes accessed | tf_op | source)
XLA Modules:
  0.0 78.5 jit_solution(844963495073492451)
XLA Ops:
  0.0 0.0 copy-start.4
  0.0 0.7 copy-done.4
  0.7 0.0 copy-start.5
  0.7 0.1 reshape_squeeze.6
  0.8 0.5 broadcast.5
  1.3 0.1 copy-done.5
  1.4 0.0 copy-start.6
  1.4 0.7 reduce.3
  2.0 0.0 copy-start.3
  2.1 0.1 reshape_squeeze.7
  2.1 0.0 copy-done.6
  2.1 0.1 pad_add_fusion.1
  2.2 0.5 copy-done.3
  2.7 0.0 copy-start
  2.7 1.2 %copy-done = f32[256,1024]{1,0:T(8,128)S(1)} copy-done((f32[256,1024]{1,0:T(8,128)S(1)}, f32[256,1024]{1,0:T(8,128)}, u32[]{:S(2)}) %copy-start) | copy-done | bytes 1048600
  4.0 0.0 copy-start.1
  4.0 1.2 %copy-done.1 = f32[256,1024]{1,0:T(8,128)S(1)} copy-done((f32[256,1024]{1,0:T(8,128)S(1)}, f32[256,1024]{1,0:T(8,128)}, u32[]{:S(2)}) %copy-start.1) | copy-done | bytes 1048600
  5.2 0.0 copy-start.2
  5.2 1.1 %copy-done.2 = bf16[1,4,6,128,128]{4,3,2,1,0:T(8,128)(2,1)S(1)} copy-done((bf16[1,4,6,128,128]{4,3,2,1,0:T(8,128)(2,1)S(1)}, bf16[1,4,6,128,128]{4,3,2,1,0:T(8,128)(2,1)}, u32[]{:S(2)}) %copy-start.2) | copy-done | bytes 786456
  6.3 71.2 %shard_map.73 = f32[256,1024]{1,0:T(8,128)S(1)} custom-call(f32[256,1024]{1,0:T(8,128)S(1)} %copy-done, f32[256,1024]{1,0:T(8,128)S(1)} %copy-done.1, bf16[4,6,128,128]{3,2,1,0:T(8,128)(2,1)S(1)} %bitcast.5, s32[16,128]{1,0:T(8,128)S(1)} %pad_add_fusion.info), custom_call_target="tpu_custom_call" | custom-call | tf_op jit(solution)/shard_map/pallas_call | solution.py:394
  77.5 1.0 %copy.9 = f32[256,1024]{1,0:T(8,128)} copy(f32[256,1024]{1,0:T(8,128)S(1)} %shard_map.73) | data formatting | bytes 2097152
  (2 shorter events, 0.0 us)
Async XLA Ops:
  0.0 0.7 copy-start.4
  0.7 0.7 copy-start.5
  1.4 0.8 copy-start.6
  2.0 0.7 copy-start.3
  2.7 1.2 %copy-start = (f32[256,1024]{1,0:T(8,128)S(1)}, f32[256,1024]{1,0:T(8,128)}, u32[]{:S(2)}) copy-start(f32[256,1024]{1,0:T(8,128)} %scores.1) | copy-start | bytes 3145732
  4.0 1.2 %copy-start.1 = (f32[256,1024]{1,0:T(8,128)S(1)}, f32[256,1024]{1,0:T(8,128)}, u32[]{:S(2)}) copy-start(f32[256,1024]{1,0:T(8,128)} %prior.1) | copy-start | bytes 3145732
  5.2 1.1 %copy-start.2 = (bf16[1,4,6,128,128]{4,3,2,1,0:T(8,128)(2,1)S(1)}, bf16[1,4,6,128,128]{4,3,2,1,0:T(8,128)(2,1)}, u32[]{:S(2)}) copy-start(bf16[1,4,6,128,128]{4,3,2,1,0:T(8,128)(2,1)} %param.9) | copy-start | bytes 2359300

commit v2 on v1

--- a/solution.py
+++ b/solution.py
@@ -10,6 +10,9 @@
 CLASSES = 1024
 ITERS = 2
 MESH = pl.DeviceIdType.MESH
+PIECES = 3
+LAG = 3
+FIRST = 3
 F32 = jnp.float32
 I32 = jnp.int32
 
@@ -80,11 +83,12 @@
 
 def kernel(
     N, C, NB, CAP, RT,
-    scores, prior, tiles, info, out,
+    scores_in, prior_in, tiles, col_tile, row_tile, counts, seeds_in, out,
+    scores, prior, info,
     words, rx_words, pwords, rx_pwords, owords, rx_owords,
     all_tiles, field, low, votes, rx_info, sm,
     sums, rx_sums, csums, rx_csums, total, side, rx_side, osum, rx_osum, mine,
-    local_sem, sm_sem,
+    local_sem, scores_sem, prior_sem, sm_sem,
     info_s, info_r, tz_s, tz_r, tx_s, tx_r, tc_s, tc_r, td_s, td_r,
     sc_s, sc_r, pr_s, pr_r, c1_s, c1_r, z1_s, z1_r, sd_s, sd_r, o_s, o_r, c2_s, c2_r,
 ):
@@ -109,6 +113,8 @@
     kpeer = c + 1 - 2 * lax.rem(c, 2)
     xkpeer = lax.rem(kpeer + 2, C)
     order = [2, 1, 3]
+    waiting = [1, 3, 2]
+    PIECE = CAP // PIECES
 
     def remote(src, dst, s, r, **to):
         return pltpu.make_async_remote_copy(
@@ -121,30 +127,78 @@
     for k in range(1, C):
         pl.semaphore_signal(barrier, inc=1, device_id={"classes": cnode(k)}, device_id_type=MESH)
 
+    load_scores = pltpu.make_async_copy(scores_in, scores, scores_sem)
+    load_scores.start()
     own_tiles = pltpu.make_async_copy(tiles, all_tiles.at[n], local_sem)
     own_tiles.start()
+    load_prior = pltpu.make_async_copy(prior_in, prior, prior_sem)
+    load_prior.start()
+
+    lane = lax.broadcasted_iota(I32, (8, 128), 1)
+    line = jnp.zeros((8, 128), I32)
+    for d in range(N):
+        for s in range(CAP):
+            line = jnp.where(lane == d * CAP + s, col_tile[0, d, s], line)
+            line = jnp.where(lane == SL + d * CAP + s, row_tile[d, 0, s], line)
+        line = jnp.where(lane == 2 * SL + d, counts[d], line)
+    info[0:8] = line
+    info[8:16] = seeds_in[...]
     rx_info[n] = info[...]
 
-    def code_scores(d, carry):
-        rows = pl.ds(pl.multiple_of(d * RT, RT), RT)
-        for b in range(NB):
-            words[d, b] = pack(encode_scores(scores[rows, b * 128:(b + 1) * 128]))
-        return carry
-
-    lax.fori_loop(0, N, code_scores, 0)
+    pieces = [(h, k) for h in range(PIECES) for k in waiting]
+
+    def piece(p, q, h):
+        return all_tiles.at[p, q, pl.ds(h * PIECE, PIECE)]
+
+    def tile_z(h, k):
+        i = h * N + k
+        return remote(
+            tiles.at[c, pl.ds(h * PIECE, PIECE)], piece(n, c, h), tz_s.at[i], tz_r.at[i], nodes=znode(k)
+        )
+
+    def tile_x(h, k):
+        i = h * N + k
+        here = piece(zfrom(k), c, h)
+        return remote(here, here, tx_s.at[i], tx_r.at[i], classes=xpeer)
+
+    def tile_c(h, k):
+        i = h * N + k
+        here = piece(zfrom(k), c, h)
+        return remote(here, here, tc_s.at[i], tc_r.at[i], classes=kpeer)
+
+    def tile_d(h, k):
+        i = h * N + k
+        here = piece(zfrom(k), xpeer, h)
+        return remote(here, here, td_s.at[i], td_r.at[i], classes=kpeer)
+
     pl.semaphore_wait(barrier, N - 1 + C - 1)
-
     infos = [remote(info, rx_info.at[n], info_s.at[k], info_r.at[k], nodes=znode(k)) for k in order]
-    tzs = [
-        remote(tiles.at[c], all_tiles.at[n, c], tz_s.at[k], tz_r.at[k], nodes=znode(k))
-        for k in order
-    ]
-    scs = [
-        remote(words.at[znode(k)], rx_words.at[n], sc_s.at[k], sc_r.at[k], nodes=znode(k))
-        for k in order
-    ]
-    for copy in infos + tzs + scs:
-        copy.start()
+    tzs = [tile_z(h, k) for h, k in pieces]
+    for copy in infos + tzs[:FIRST]:
+        copy.start()
+
+    load_scores.wait()
+    scs = []
+    for k in order:
+        d = znode(k)
+
+        def code_scores(b, carry):
+            rows = pl.ds(pl.multiple_of(d * RT, RT), RT)
+            cols = pl.ds(pl.multiple_of(b * 128, 128), 128)
+            words[d, b] = pack(encode_scores(scores[rows, cols]))
+            return carry
+
+        lax.fori_loop(0, NB, code_scores, 0)
+        scs.append(remote(words.at[d], rx_words.at[n], sc_s.at[k], sc_r.at[k], nodes=d))
+        scs[-1].start()
+    for copy in tzs[FIRST:]:
+        copy.start()
+
+    own_rows = pl.ds(pl.multiple_of(n * RT, RT), RT)
+    for b in range(NB):
+        x = scores[own_rows, b * 128:(b + 1) * 128]
+        field[n * NB + b] = x
+        low[n * NB + b] = x.astype(jnp.bfloat16)
 
     def code_prior(d, carry):
         rows = pl.ds(pl.multiple_of(d * RT, RT), RT)
@@ -154,34 +208,37 @@
             )
         return carry
 
+    load_prior.wait()
     lax.fori_loop(0, N, code_prior, 0)
+    rx_pwords[n] = pwords[n]
+
+    txs, tcs, tds = [], [], []
+
+    def relay_x(h, k):
+        i = h * N + k
+        here = piece(zfrom(k), xpeer, h)
+        remote(here, here, tx_s.at[i], tx_r.at[i], classes=xpeer).wait_recv()
+        tds.append(tile_d(h, k))
+        tds[-1].start()
+
+    for i, (h, k) in enumerate(pieces):
+        j = h * N + k
+        here = piece(zfrom(k), c, h)
+        remote(here, here, tz_s.at[j], tz_r.at[j], nodes=zfrom(k)).wait_recv()
+        txs.append(tile_x(h, k))
+        txs[-1].start()
+        tcs.append(tile_c(h, k))
+        tcs[-1].start()
+        if i >= LAG:
+            relay_x(*pieces[i - LAG])
     prs = [
         remote(pwords.at[znode(k)], rx_pwords.at[n], pr_s.at[k], pr_r.at[k], nodes=znode(k))
         for k in order
     ]
     for copy in prs:
         copy.start()
-
-    own_rows = pl.ds(pl.multiple_of(n * RT, RT), RT)
-    for b in range(NB):
-        x = scores[own_rows, b * 128:(b + 1) * 128]
-        field[n * NB + b] = x
-        low[n * NB + b] = x.astype(jnp.bfloat16)
-    rx_pwords[n] = pwords[n]
-
-    waiting = [1, 3, 2]
-    txs, tcs, tds = [], [], []
-    for k in waiting:
-        p = zfrom(k)
-        remote(tiles.at[c], all_tiles.at[p, c], tz_s.at[k], tz_r.at[k], nodes=p).wait_recv()
-        txs.append(
-            remote(all_tiles.at[p, c], all_tiles.at[p, c], tx_s.at[k], tx_r.at[k], classes=xpeer)
-        )
-        tcs.append(
-            remote(all_tiles.at[p, c], all_tiles.at[p, c], tc_s.at[k], tc_r.at[k], classes=kpeer)
-        )
-        txs[-1].start()
-        tcs[-1].start()
+    for h, k in pieces[-LAG:]:
+        relay_x(h, k)
     for k in order:
         remote(info, rx_info.at[zfrom(k)], info_s.at[k], info_r.at[k], nodes=zfrom(k)).wait_recv()
     to_sm = pltpu.make_async_copy(rx_info.at[:, 0:8], sm, sm_sem)
@@ -199,37 +256,18 @@
         lax.fori_loop(0, NB, take_scores, 0)
     to_sm.wait()
     own_tiles.wait()
-    for k in waiting:
-        p = zfrom(k)
-        remote(
-            all_tiles.at[p, xpeer], all_tiles.at[p, xpeer], tx_s.at[k], tx_r.at[k], classes=xpeer
-        ).wait_recv()
-        tds.append(
-            remote(
-                all_tiles.at[p, xpeer], all_tiles.at[p, xpeer], td_s.at[k], td_r.at[k], classes=kpeer
-            )
-        )
-        tds[-1].start()
-    for k in waiting:
-        p = zfrom(k)
-        remote(
-            all_tiles.at[p, kpeer], all_tiles.at[p, kpeer], tc_s.at[k], tc_r.at[k], classes=kpeer
-        ).wait_recv()
-        remote(
-            all_tiles.at[p, xkpeer], all_tiles.at[p, xkpeer], td_s.at[k], td_r.at[k], classes=kpeer
-        ).wait_recv()
+
+    def cast(p, d):
+        for s in range(CAP):
+            col = sm[p, 0, d * CAP + s]
+            block = jnp.dot(low[p * NB + col], all_tiles[p, d, s], preferred_element_type=F32)
+            votes[d * SL + p * CAP + s] = block.astype(jnp.bfloat16).astype(F32)
+
+    def cast_from(p):
+        lax.fori_loop(0, N, lambda d, carry: (cast(p, d), carry)[1], 0)
 
     def cast_votes(d):
-        def one(p, carry):
-            for s in range(CAP):
-                col = sm[p, 0, d * CAP + s]
-                block = jnp.dot(
-                    low[p * NB + col], all_tiles[p, d, s], preferred_element_type=F32
-                )
-                votes[p * CAP + s] = block.astype(jnp.bfloat16).astype(F32)
-            return carry
-
-        lax.fori_loop(0, N, one, 0)
+        lax.fori_loop(0, N, lambda p, carry: (cast(p, d), carry)[1], 0)
 
     def tally(d, b):
         acc = field[d * NB + b]
@@ -237,12 +275,20 @@
             p, s = i // CAP, i % CAP
             row = sm[d, 0, SL + i]
             hit = jnp.logical_and(row == b, s < sm[d, 0, 2 * SL + p])
-            acc = acc + jnp.where(hit, 1.0, 0.0).astype(F32) * votes[i]
+            acc = acc + jnp.where(hit, 1.0, 0.0).astype(F32) * votes[d * SL + i]
         return acc
 
+    cast_from(n)
+    for k in waiting:
+        for h in range(PIECES):
+            i = h * N + k
+            here = piece(zfrom(k), kpeer, h)
+            remote(here, here, tc_s.at[i], tc_r.at[i], classes=kpeer).wait_recv()
+            here = piece(zfrom(k), xkpeer, h)
+            remote(here, here, td_s.at[i], td_r.at[i], classes=kpeer).wait_recv()
+        cast_from(zfrom(k))
+
     def first(d, carry):
-        cast_votes(d)
-
         def one(b, carry):
             acc = tally(d, b)
             field[d * NB + b] = acc
@@ -370,6 +416,7 @@
         and scores.shape[1] // tiles.shape[-1] == 8
         and tiles.shape[-1] == 128
         and (scores.shape[0] // 4) % 16 == 0
+        and tiles.shape[2] % PIECES == 0
         and 2 * tiles.shape[1] * tiles.shape[2] + tiles.shape[1] <= 128
     )
 
@@ -381,27 +428,26 @@
     NB = scores.shape[1] // TW
     RT = R // N
     SL = N * CAP
-    line = jnp.concatenate(
-        [col_tile[0].reshape(-1), row_tile[:, 0].reshape(-1), counts[:, 0]]
-    )
-    line = jnp.pad(line, (0, 8 * TW - line.shape[0])).reshape(8, TW)
-    info = jnp.concatenate([line, seed_mask.reshape(NB, TW)], axis=0)
     V = pltpu.VMEM
     words = V((N, NB, RT // 2, TW), I32)
     dma = pltpu.SemaphoreType.DMA
-    pairs = [dma((4,)) for _ in range(24)]
+    sems = [4] * 2 + [4 * PIECES] * 8 + [4] * 14
+    pairs = [dma((size,)) for size in sems]
+    smem = pl.BlockSpec(memory_space=pltpu.SMEM)
+    anywhere = pl.BlockSpec(memory_space=pl.ANY)
     vm = pl.BlockSpec(memory_space=pltpu.VMEM)
     return pl.pallas_call(
         functools.partial(kernel, N, C, NB, CAP, RT),
         out_shape=jax.ShapeDtypeStruct(scores.shape, F32),
-        in_specs=[vm] * 4,
+        in_specs=[anywhere] * 3 + [smem] * 3 + [vm],
         out_specs=vm,
         scratch_shapes=[
+            V(scores.shape, F32), V(scores.shape, F32), V((16, TW), I32),
             words, words, words, words, words, words,
             V((N, N, CAP, TW, TW), jnp.bfloat16),
             V((N * NB, RT, TW), F32),
             V((N * NB, RT, TW), jnp.bfloat16),
-            V((SL, RT, TW), F32),
+            V((N * SL, RT, TW), F32),
             V((N, 16, TW), I32),
             pltpu.SMEM((N, 8, TW), I32),
             V((N, NB, TW), F32),
@@ -414,14 +460,13 @@
             V((NB, TW), F32),
             V((C, NB, TW), F32),
             V((NB, RT, TW), F32),
-            dma,
-            dma,
+            dma, dma, dma, dma,
             *pairs,
         ],
         compiler_params=pltpu.CompilerParams(
-            collective_id=0, has_side_effects=True, vmem_limit_bytes=40 * 1024 * 1024
+            collective_id=0, has_side_effects=True, vmem_limit_bytes=60 * 1024 * 1024
         ),
-    )(scores, prior, tiles[0], info)
+    )(scores, prior, tiles[0], col_tile, row_tile, counts[:, 0], seed_mask.reshape(NB, TW))
 
 
 def solution(mesh):

time: 78.8 us -> 73.1 us (0.928)
  local copies, waits for them, and re-layouts: 6.52 us -> 2.31 us
    unnamed x16 -> x1, local copies, waits for them, and re-layouts: 6.35 us -> 2.31 us
where the time goes in v2:
time: 73.1 us; the launch traced here: 72.9 us
  Pallas kernels  70.6 us (97%)
  local copies, waits for them, and re-layouts  2.31 us (3%)
    pallas_call x1, Pallas kernels, transposed(): pl.pallas_call(functools.partial(kernel, N, C, NB, CAP, RT), out_shape=ja...  70.6 us
    unnamed x1, local copies, waits for them, and re-layouts  2.31 us

profile of v2, /device:TPU:13, one launch (start us, length us, event | category | flops | bytes accessed | tf_op | source)
XLA Modules:
  0.0 72.9 jit_solution(5087173110967561669)
XLA Ops:
  0.0 70.6 %shard_map.73 = f32[256,1024]{1,0:T(8,128)} custom-call(f32[256,1024]{1,0:T(8,128)} %scores_in.1, f32[256,1024]{1,0:T(8,128)} %prior_in.1, bf16[4,6,128,128]{3,2,1,0:T(8,128)(2,1)} %bitcast.3, s32[1,4,6]{2,1,0:T(4,128)} %col_tile.1, s32[4,1,6]{2,1,0:T(1,128)} %row_tile.1, s32[4]{0:T(128)} %bitcast.5, s32[8,128]{1,0:T(8,128)} %bitcast.4), custom_call_target="tpu_custom_call" | custom-call | tf_op jit(solution)/shard_map/pallas_call | solution.py:439
  70.6 2.3 %copy.9 = f32[256,1024]{1,0:T(8,128)} copy(f32[256,1024]{1,0:T(8,128)} %shard_map.73) | data formatting | bytes 2097152

commit v3 on v2

--- a/solution.py
+++ b/solution.py
@@ -12,7 +12,6 @@
 MESH = pl.DeviceIdType.MESH
 PIECES = 3
 LAG = 3
-FIRST = 3
 F32 = jnp.float32
 I32 = jnp.int32
 
@@ -89,7 +88,7 @@
     all_tiles, field, low, votes, rx_info, sm,
     sums, rx_sums, csums, rx_csums, total, side, rx_side, osum, rx_osum, mine,
     local_sem, scores_sem, prior_sem, sm_sem,
-    info_s, info_r, tz_s, tz_r, tx_s, tx_r, tc_s, tc_r, td_s, td_r,
+    info_s, info_r, tz_s, tz_r, tf_s, tx_s, tx_r, tc_s, tc_r, td_s, td_r,
     sc_s, sc_r, pr_s, pr_r, c1_s, c1_r, z1_s, z1_r, sd_s, sd_r, o_s, o_r, c2_s, c2_r,
 ):
     n = lax.axis_index("nodes")
@@ -145,16 +144,40 @@
     info[8:16] = seeds_in[...]
     rx_info[n] = info[...]
 
-    pieces = [(h, k) for h in range(PIECES) for k in waiting]
+    first_end, last_end = n == 0, n == N - 1
+    near = [
+        jnp.where(first_end, 3, 1),
+        jnp.where(jnp.logical_or(first_end, last_end), 2, 3),
+        jnp.where(first_end, 1, jnp.where(last_end, 3, 2)),
+    ]
+    pieces = [(h, k) for h in range(PIECES) for k in near[:2]]
+    pieces += [(h, near[2]) for h in range(PIECES)]
 
     def piece(p, q, h):
         return all_tiles.at[p, q, pl.ds(h * PIECE, PIECE)]
 
-    def tile_z(h, k):
-        i = h * N + k
+    def tile_up(h):
+        i = h * N + 1
         return remote(
-            tiles.at[c, pl.ds(h * PIECE, PIECE)], piece(n, c, h), tz_s.at[i], tz_r.at[i], nodes=znode(k)
+            tiles.at[c, pl.ds(h * PIECE, PIECE)], piece(n, c, h), tz_s.at[i], tz_r.at[i], nodes=up
         )
+
+    def tile_down(h):
+        i = h * N + 3
+        return remote(
+            tiles.at[c, pl.ds(h * PIECE, PIECE)], piece(n, c, h), tz_s.at[i], tz_r.at[i], nodes=down
+        )
+
+    up, down = lax.rem(n + 1, N), lax.rem(n + N - 1, N)
+
+    def onward(h, k):
+        p = zfrom(k)
+        rising = p < n
+        here = piece(p, c, h)
+        to = jnp.where(rising, up, down)
+        there = h * N + lax.rem(to - p + N, N)
+        going = jnp.where(rising, n < N - 1, n > 0)
+        return going, remote(here, here, tf_s.at[h * N + k], tz_r.at[there], nodes=to)
 
     def tile_x(h, k):
         i = h * N + k
@@ -173,9 +196,11 @@
 
     pl.semaphore_wait(barrier, N - 1 + C - 1)
     infos = [remote(info, rx_info.at[n], info_s.at[k], info_r.at[k], nodes=znode(k)) for k in order]
-    tzs = [tile_z(h, k) for h, k in pieces]
-    for copy in infos + tzs[:FIRST]:
+    for copy in infos:
         copy.start()
+    for h in range(PIECES):
+        pl.when(n < N - 1)(lambda h=h: tile_up(h).start())
+        pl.when(n > 0)(lambda h=h: tile_down(h).start())
 
     load_scores.wait()
     scs = []
@@ -191,8 +216,6 @@
         lax.fori_loop(0, NB, code_scores, 0)
         scs.append(remote(words.at[d], rx_words.at[n], sc_s.at[k], sc_r.at[k], nodes=d))
         scs[-1].start()
-    for copy in tzs[FIRST:]:
-        copy.start()
 
     own_rows = pl.ds(pl.multiple_of(n * RT, RT), RT)
     for b in range(NB):
@@ -225,6 +248,8 @@
         j = h * N + k
         here = piece(zfrom(k), c, h)
         remote(here, here, tz_s.at[j], tz_r.at[j], nodes=zfrom(k)).wait_recv()
+        going, copy = onward(h, k)
+        pl.when(going)(copy.start)
         txs.append(tile_x(h, k))
         txs[-1].start()
         tcs.append(tile_c(h, k))
@@ -279,7 +304,7 @@
         return acc
 
     cast_from(n)
-    for k in waiting:
+    for k in near:
         for h in range(PIECES):
             i = h * N + k
             here = piece(zfrom(k), kpeer, h)
@@ -405,7 +430,13 @@
             codes = unpack(rx_owords[p, b]).astype(F32)
             finish(p, b, codes * rx_side[p, 8 + b:9 + b])
 
-    for copy in infos + tzs + scs + prs + txs + tcs + tds + c1s + z1s + sds + outs + c2s:
+    for h in range(PIECES):
+        pl.when(n < N - 1)(lambda h=h: tile_up(h).wait_send())
+        pl.when(n > 0)(lambda h=h: tile_down(h).wait_send())
+    for h, k in pieces:
+        going, copy = onward(h, k)
+        pl.when(going)(copy.wait_send)
+    for copy in infos + scs + prs + txs + tcs + tds + c1s + z1s + sds + outs + c2s:
         copy.wait_send()
 
 
@@ -431,7 +462,7 @@
     V = pltpu.VMEM
     words = V((N, NB, RT // 2, TW), I32)
     dma = pltpu.SemaphoreType.DMA
-    sems = [4] * 2 + [4 * PIECES] * 8 + [4] * 14
+    sems = [4] * 2 + [4 * PIECES] * 9 + [4] * 14
     pairs = [dma((size,)) for size in sems]
     smem = pl.BlockSpec(memory_space=pltpu.SMEM)
     anywhere = pl.BlockSpec(memory_space=pl.ANY)

time: 73.1 us -> 70.4 us (0.963)
  Pallas kernels: 70.6 us -> 67.9 us
    pallas_call x1, Pallas kernels: 70.6 us -> 67.9 us  [transposed(): pl.pallas_call(functools.partial(kernel, N, C, NB, CAP, RT), out_shape=ja...]
where the time goes in v3:
time: 70.4 us; the launch traced here: 70.2 us
  Pallas kernels  67.9 us (96%)
  local copies, waits for them, and re-layouts  2.31 us (3%)
    pallas_call x1, Pallas kernels, transposed(): pl.pallas_call(functools.partial(kernel, N, C, NB, CAP, RT), out_shape=ja...  67.9 us
    unnamed x1, local copies, waits for them, and re-layouts  2.31 us

profile of v3, /device:TPU:13, one launch (start us, length us, event | category | flops | bytes accessed | tf_op | source)
XLA Modules:
  0.0 70.2 jit_solution(17528257761762050840)
XLA Ops:
  0.0 67.9 %shard_map.73 = f32[256,1024]{1,0:T(8,128)} custom-call(f32[256,1024]{1,0:T(8,128)} %scores_in.1, f32[256,1024]{1,0:T(8,128)} %prior_in.1, bf16[4,6,128,128]{3,2,1,0:T(8,128)(2,1)} %bitcast.3, s32[1,4,6]{2,1,0:T(4,128)} %col_tile.1, s32[4,1,6]{2,1,0:T(1,128)} %row_tile.1, s32[4]{0:T(128)} %bitcast.5, s32[8,128]{1,0:T(8,128)} %bitcast.4), custom_call_target="tpu_custom_call" | custom-call | tf_op jit(solution)/shard_map/pallas_call | solution.py:470
  67.9 2.3 %copy.9 = f32[256,1024]{1,0:T(8,128)} copy(f32[256,1024]{1,0:T(8,128)} %shard_map.73) | data formatting | bytes 2097152

commit v4 on v3

--- a/solution.py
+++ b/solution.py
@@ -256,12 +256,6 @@
         tcs[-1].start()
         if i >= LAG:
             relay_x(*pieces[i - LAG])
-    prs = [
-        remote(pwords.at[znode(k)], rx_pwords.at[n], pr_s.at[k], pr_r.at[k], nodes=znode(k))
-        for k in order
-    ]
-    for copy in prs:
-        copy.start()
     for h, k in pieces[-LAG:]:
         relay_x(h, k)
     for k in order:
@@ -279,6 +273,12 @@
             return carry
 
         lax.fori_loop(0, NB, take_scores, 0)
+    prs = [
+        remote(pwords.at[znode(k)], rx_pwords.at[n], pr_s.at[k], pr_r.at[k], nodes=znode(k))
+        for k in order
+    ]
+    for copy in prs:
+        copy.start()
     to_sm.wait()
     own_tiles.wait()
 
@@ -289,10 +289,10 @@
             votes[d * SL + p * CAP + s] = block.astype(jnp.bfloat16).astype(F32)
 
     def cast_from(p):
-        lax.fori_loop(0, N, lambda d, carry: (cast(p, d), carry)[1], 0)
+        lax.fori_loop(0, N, lambda d, carry: (cast(p, d), carry)[1], 0, unroll=True)
 
     def cast_votes(d):
-        lax.fori_loop(0, N, lambda p, carry: (cast(p, d), carry)[1], 0)
+        lax.fori_loop(0, N, lambda p, carry: (cast(p, d), carry)[1], 0, unroll=True)
 
     def tally(d, b):
         acc = field[d * NB + b]

time: 70.4 us -> 65.1 us (0.925)
  Pallas kernels: 67.9 us -> 62.6 us
    pallas_call x1, Pallas kernels: 67.9 us -> 62.6 us  [transposed(): pl.pallas_call(functools.partial(kernel, N, C, NB, CAP, RT), out_shape=ja...]
where the time goes in v4:
time: 65.1 us; the launch traced here: 64.9 us
  Pallas kernels  62.6 us (96%)
  local copies, waits for them, and re-layouts  2.31 us (4%)
    pallas_call x1, Pallas kernels, transposed(): pl.pallas_call(functools.partial(kernel, N, C, NB, CAP, RT), out_shape=ja...  62.6 us
    unnamed x1, local copies, waits for them, and re-layouts  2.31 us

profile of v4, /device:TPU:13, one launch (start us, length us, event | category | flops | bytes accessed | tf_op | source)
XLA Modules:
  0.0 64.9 jit_solution(611041944819582046)
XLA Ops:
  0.0 62.6 %shard_map.73 = f32[256,1024]{1,0:T(8,128)} custom-call(f32[256,1024]{1,0:T(8,128)} %scores_in.1, f32[256,1024]{1,0:T(8,128)} %prior_in.1, bf16[4,6,128,128]{3,2,1,0:T(8,128)(2,1)} %bitcast.3, s32[1,4,6]{2,1,0:T(4,128)} %col_tile.1, s32[4,1,6]{2,1,0:T(1,128)} %row_tile.1, s32[4]{0:T(128)} %bitcast.5, s32[8,128]{1,0:T(8,128)} %bitcast.4), custom_call_target="tpu_custom_call" | custom-call | tf_op jit(solution)/shard_map/pallas_call | solution.py:470
  62.6 2.3 %copy.9 = f32[256,1024]{1,0:T(8,128)} copy(f32[256,1024]{1,0:T(8,128)} %shard_map.73) | data formatting | bytes 2097152
